TPU v7x, 32 devices: a whole 2x2x4 slice. The times are simulated.
32 devices in a mesh: horiz: 8 (over z, y), vert: 4 (over x, core).
Axes of the slice: x: 2, y: 2, z: 4, core: 2. Of those that a mesh axis runs over, the one named last changes fastest.
Arguments:
- tracer: bfloat16 [8, 2048, 128], P('vert', 'horiz'), may hold values from -6 to 6
- explicit_tiles: bfloat16 [8, 16, 7, 128, 128], P('vert', 'horiz'), may hold values from -0.25 to 0.25
- tile_columns: int32 [8, 16, 7], P('vert', 'horiz'), may hold values from 0 to 127, as said below
- tile_counts: int32 [8, 16], P('vert', 'horiz'), may hold values from 4 to 7
- surface_source: bfloat16 [2048, 128], P('horiz'), may hold values from -6 to 6
- implicit_columns: float32 [2048, 8, 8], P(('horiz', 'vert')), may hold values from -0.53033009 to 1
- settling: float32 [128], replicated, may hold values from 0.02 to 0.5
- wet_mask: int32 [8, 2048], P('vert', 'horiz'), may hold values 0 or 1
Outputs:
- tracer_out: bfloat16 [8, 2048, 128], P('vert', 'horiz')
Inputs may be any that keep to these rules, and one draw needn't show every extreme that they name: `tile_columns`: slot 0 of block row (l, t) names the row's own tile l * 16 + t; the other slots name distinct tiles within 2 levels and 2 tiles of it, inside the grid.
All inputs are finite; a program needn't handle non-finite values. No bound on the sum of `wet_mask` on one device may be relied on, other than what follows from the above.
Results may differ from a plain program's by a relative error of at most 0.015.
Values may be sent and summed in bfloat16 or wider, within the bound.
A program may use at most 64 MiB of HBM per device.

v0:
```python
import jax
import jax.numpy as jnp
from jax import lax
from jax.sharding import PartitionSpec as P

REACH = 2
STEPS = 4


def extended(shard, sides, width):
    for axis, dim in sides:
        size, length = (lax.axis_size(axis), shard.shape[dim])
        up = [(i, (i + 1) % size) for i in range(size - 1)]
        down = [(j, i) for i, j in up]
        last = lax.slice_in_dim(shard, length - width, length, axis=dim)
        leading = lax.slice_in_dim(shard, 0, width, axis=dim)
        before = lax.ppermute(last, axis, up)
        after = lax.ppermute(leading, axis, down)
        shard = jnp.concatenate([before, shard, after], axis=dim)
    return shard


def from_behind(value, axis, steps):
    count = lax.axis_size(axis)
    leading, last = (max(0, -steps), min(count, count - steps))
    return lax.ppermute(value, axis, [(source, source + steps) for source in range(leading, last)])


def on_device(
    tracer,
    explicit_tiles,
    tile_columns,
    tile_counts,
    surface_source,
    implicit_columns,
    settling,
    wet_mask,
):
    lev_dev, cells_dev, classes = tracer.shape
    tile_size = explicit_tiles.shape[-1]
    tiles_dev = cells_dev // tile_size
    slot_count = explicit_tiles.shape[2]
    h_tiles = tiles_dev * lax.axis_size("horiz")
    wide_tiles = tiles_dev + 2 * REACH
    first_level = lax.axis_index("vert") * lev_dev
    first_tile = lax.axis_index("horiz") * tiles_dev
    col_level = tile_columns // h_tiles - (first_level - REACH)
    col_tile = tile_columns % h_tiles - (first_tile - REACH)
    position = col_level * wide_tiles + col_tile
    live_slots = (
        jnp.arange(slot_count, dtype=jnp.int32)[None, None, :] < tile_counts[:, :, None]
    ).astype(jnp.bfloat16)
    on_top = first_level + jnp.arange(lev_dev, dtype=jnp.int32) == 0
    source = surface_source.astype(jnp.float32)
    fall_rate = settling[None, None, :]
    wet_cells = wet_mask.astype(jnp.bfloat16)[:, :, None]
    all_columns = lax.all_gather(implicit_columns, "vert", axis=0, tiled=True)
    own_rows = lax.dynamic_slice_in_dim(all_columns, first_level, lev_dev, 1)
    current = tracer
    for step_index in range(STEPS):
        slab_grid = current.reshape(lev_dev, tiles_dev, tile_size, classes)
        padded = extended(slab_grid, (("horiz", 1), ("vert", 0)), REACH)
        flattened = padded.reshape(-1, tile_size, classes)
        picked = flattened[position] * live_slots[:, :, :, None, None]
        explicit_flow = jnp.einsum(
            "ltjab,ltjbs->ltas", explicit_tiles, picked, preferred_element_type=jnp.float32
        )
        explicit_flow = explicit_flow.reshape(lev_dev, cells_dev, classes)
        explicit_flow = explicit_flow + jnp.where(on_top[:, None, None], source[None, :, :], 0.0)
        loaded = explicit_flow.astype(jnp.bfloat16)
        mixed_col = jnp.einsum(
            "ckm,mcs->kcs",
            own_rows,
            lax.all_gather(loaded, "vert", axis=0, tiled=True).astype(jnp.float32),
            precision=lax.Precision.HIGHEST,
        )
        upper_level = from_behind(mixed_col[-1].astype(jnp.bfloat16), "vert", 1).astype(jnp.float32)
        from_above = jnp.concatenate([upper_level[None], mixed_col[:-1]], axis=0)
        settled = (1.0 - fall_rate) * mixed_col + fall_rate * from_above
        current = (settled * wet_cells.astype(jnp.float32)).astype(jnp.bfloat16)
    return current


def solution(mesh):
    placed = (
        P("vert", "horiz", None),
        P("vert", "horiz", None, None, None),
        P("vert", "horiz", None),
        P("vert", "horiz"),
        P("horiz", None),
        P(("horiz", "vert"), None, None),
        P(),
        P("vert", "horiz"),
    )
    return jax.shard_map(
        on_device, mesh=mesh, in_specs=placed, out_specs=P("vert", "horiz", None), check_vma=False
    )
```

profile of v0, /device:TPU:25, one launch (start us, length us, event | category | flops | bytes accessed | tf_op | source)
XLA Modules:
  0.0 165.3 jit_solution(6005104641196930024)
XLA Ops:
  0.0 3.2 %collective-permute-start.1 = (bf16[2,2,128,128]{3,2,1,0:T(8,128)(2,1)}, bf16[2,2,128,128]{3,2,1,0:T(8,128)(2,1)S(1)}, u32[]{:S(2)}, u32[]{:S(2)}) collective-permute-start(bf16[2,2,128,128]{3,2,1,0:T(8,128)(2,1)} %bitcast.82), channel_id=1, source_target_pairs={{4,0},{8,4},{12,8},{16,12},{20,16},{24,20},{28,24},{5,1},{9,5},{13... | collective-permute-start | bytes 393224 | tf_op jit(solution)/shard_map/ppermute | solution.py:18
  3.2 2.3 %collective-permute-start = (bf16[2,2,128,128]{3,2,1,0:T(8,128)(2,1)}, bf16[2,2,128,128]{3,2,1,0:T(8,128)(2,1)S(1)}, u32[]{:S(2)}, u32[]{:S(2)}) collective-permute-start(bf16[2,2,128,128]{3,2,1,0:T(8,128)(2,1)} %bitcast.83), channel_id=1, source_target_pairs={{0,4},{4,8},{8,12},{12,16},{16,20},{20,24},{24,28},{1,5},{5,9},{9,... | collective-permute-start | bytes 393224 | tf_op jit(solution)/shard_map/ppermute | solution.py:17
  8.0 11.1 %all_gather.16 = f32[256,8,8]{2,1,0:T(8,128)S(1)} all-gather(f32[64,8,8]{2,1,0:T(8,128)S(1)} %copy.38), channel_id=1, replica_groups=mesh['horiz'=8,'vert'=4] {'vert'}, dimensions={0}, use_global_device_ids=true | all-gather | bytes 81920 | tf_op jit(solution)/shard_map/all_gather | solution.py:57
  19.2 2.1 %collective-permute-start.3 = (bf16[2,6,128,128]{3,2,1,0:T(8,128)(2,1)S(1)}, bf16[2,6,128,128]{3,2,1,0:T(8,128)(2,1)S(1)}, u32[]{:S(2)}, u32[]{:S(2)}) collective-permute-start(bf16[2,6,128,128]{3,2,1,0:T(8,128)(2,1)S(1)} %pad_maximum_fusion.4), channel_id=1, source_target_pairs={{1,0},{2,1},{3,2},{5,4},{6,5},{7,6},{9,8},{10,9},{11,10},{13,12},{... | collective-permute-start | bytes 1179656 | tf_op jit(solution)/shard_map/ppermute | solution.py:18
  21.3 3.5 %collective-permute-start.2 = (bf16[2,6,128,128]{3,2,1,0:T(8,128)(2,1)S(1)}, bf16[2,6,128,128]{3,2,1,0:T(8,128)(2,1)S(1)}, u32[]{:S(2)}, u32[]{:S(2)}) collective-permute-start(bf16[2,6,128,128]{3,2,1,0:T(8,128)(2,1)S(1)} %pad_maximum_fusion.4), channel_id=1, source_target_pairs={{0,1},{1,2},{2,3},{4,5},{5,6},{6,7},{8,9},{9,10},{10,11},{12,13},{... | collective-permute-start | bytes 1179656 | tf_op jit(solution)/shard_map/ppermute | solution.py:17
  24.9 3.4 %collective-permute-done.3 = bf16[2,6,128,128]{3,2,1,0:T(8,128)(2,1)S(1)} collective-permute-done((bf16[2,6,128,128]{3,2,1,0:T(8,128)(2,1)S(1)}, bf16[2,6,128,128]{3,2,1,0:T(8,128)(2,1)S(1)}, u32[]{:S(2)}, u32[]{:S(2)}) %collective-permute-start.3) | collective-permute-done | bytes 393248 | tf_op jit(solution)/shard_map/ppermute | solution.py:18
  34.0 8.4 %all_gather.15 = bf16[8,256,128]{2,1,0:T(8,128)(2,1)S(1)} all-gather(bf16[2,256,128]{2,1,0:T(8,128)(2,1)S(1)} %fusion.16), channel_id=1, replica_groups=mesh['horiz'=8,'vert'=4] {'vert'}, dimensions={0}, use_global_device_ids=true | all-gather | bytes 655360 | tf_op jit(solution)/shard_map/all_gather | solution.py:74
  43.7 2.5 %collective-permute-start.4 = (bf16[256,128]{1,0:T(8,128)(2,1)S(1)}, bf16[256,128]{1,0:T(8,128)(2,1)S(1)}, u32[]{:S(2)}, u32[]{:S(2)}) collective-permute-start(bf16[256,128]{1,0:T(8,128)(2,1)S(1)} %bitcast.90), channel_id=1, source_target_pairs={{0,1},{1,2},{2,3},{4,5},{5,6},{6,7},{8,9},{9,10},{10,11},{12,13},{... | collective-permute-start | bytes 196616 | tf_op jit(solution)/shard_map/ppermute | solution.py:26
  49.9 4.3 %collective-permute-start.6 = (bf16[2,2,128,128]{3,2,1,0:T(8,128)(2,1)S(1)}, bf16[2,2,128,128]{3,2,1,0:T(8,128)(2,1)S(1)}, u32[]{:S(2)}, u32[]{:S(2)}) collective-permute-start(bf16[2,2,128,128]{3,2,1,0:T(8,128)(2,1)S(1)} %copy.42), channel_id=1, source_target_pairs={{4,0},{8,4},{12,8},{16,12},{20,16},{24,20},{28,24},{5,1},{9,5},{13... | collective-permute-start | bytes 393224 | tf_op jit(solution)/shard_map/ppermute | solution.py:18
  54.2 2.0 %collective-permute-done.5 = bf16[2,2,128,128]{3,2,1,0:T(8,128)(2,1)S(1)} collective-permute-done((bf16[2,2,128,128]{3,2,1,0:T(8,128)(2,1)S(1)}, bf16[2,2,128,128]{3,2,1,0:T(8,128)(2,1)S(1)}, u32[]{:S(2)}, u32[]{:S(2)}) %collective-permute-start.5) | collective-permute-done | bytes 131104 | tf_op jit(solution)/shard_map/ppermute | solution.py:17
  56.3 2.8 %collective-permute-done.6 = bf16[2,2,128,128]{3,2,1,0:T(8,128)(2,1)S(1)} collective-permute-done((bf16[2,2,128,128]{3,2,1,0:T(8,128)(2,1)S(1)}, bf16[2,2,128,128]{3,2,1,0:T(8,128)(2,1)S(1)}, u32[]{:S(2)}, u32[]{:S(2)}) %collective-permute-start.6) | collective-permute-done | bytes 131104 | tf_op jit(solution)/shard_map/ppermute | solution.py:18
  59.1 2.3 %collective-permute-start.8 = (bf16[2,6,128,128]{3,2,1,0:T(8,128)(2,1)S(1)}, bf16[2,6,128,128]{3,2,1,0:T(8,128)(2,1)S(1)}, u32[]{:S(2)}, u32[]{:S(2)}) collective-permute-start(bf16[2,6,128,128]{3,2,1,0:T(8,128)(2,1)S(1)} %constant_dynamic-update-slice_fusion), channel_id=1, source_target_pairs={{1,0},{2,1},{3,2},{5,4},{6,5},{7,6},{9,8},{10,9},{11,10},{13,12},{... | collective-permute-start | bytes 1179656 | tf_op jit(solution)/shard_map/ppermute | solution.py:18
  61.4 3.3 %collective-permute-start.7 = (bf16[2,6,128,128]{3,2,1,0:T(8,128)(2,1)S(1)}, bf16[2,6,128,128]{3,2,1,0:T(8,128)(2,1)S(1)}, u32[]{:S(2)}, u32[]{:S(2)}) collective-permute-start(bf16[2,6,128,128]{3,2,1,0:T(8,128)(2,1)S(1)} %constant_dynamic-update-slice_fusion), channel_id=1, source_target_pairs={{0,1},{1,2},{2,3},{4,5},{5,6},{6,7},{8,9},{9,10},{10,11},{12,13},{... | collective-permute-start | bytes 1179656 | tf_op jit(solution)/shard_map/ppermute | solution.py:17
  64.6 3.5 %collective-permute-done.8 = bf16[2,6,128,128]{3,2,1,0:T(8,128)(2,1)S(1)} collective-permute-done((bf16[2,6,128,128]{3,2,1,0:T(8,128)(2,1)S(1)}, bf16[2,6,128,128]{3,2,1,0:T(8,128)(2,1)S(1)}, u32[]{:S(2)}, u32[]{:S(2)}) %collective-permute-start.8) | collective-permute-done | bytes 393248 | tf_op jit(solution)/shard_map/ppermute | solution.py:18
  72.9 8.4 %all_gather.17 = bf16[8,256,128]{2,1,0:T(8,128)(2,1)S(1)} all-gather(bf16[2,256,128]{2,1,0:T(8,128)(2,1)S(1)} %fusion.17), channel_id=1, replica_groups=mesh['horiz'=8,'vert'=4] {'vert'}, dimensions={0}, use_global_device_ids=true | all-gather | bytes 655360 | tf_op jit(solution)/shard_map/all_gather | solution.py:74
  82.6 2.5 %collective-permute-start.9 = (bf16[256,128]{1,0:T(8,128)(2,1)S(1)}, bf16[256,128]{1,0:T(8,128)(2,1)S(1)}, u32[]{:S(2)}, u32[]{:S(2)}) collective-permute-start(bf16[256,128]{1,0:T(8,128)(2,1)S(1)} %bitcast.91), channel_id=1, source_target_pairs={{0,1},{1,2},{2,3},{4,5},{5,6},{6,7},{8,9},{9,10},{10,11},{12,13},{... | collective-permute-start | bytes 196616 | tf_op jit(solution)/shard_map/ppermute | solution.py:26
  88.8 4.3 %collective-permute-start.11 = (bf16[2,2,128,128]{3,2,1,0:T(8,128)(2,1)S(1)}, bf16[2,2,128,128]{3,2,1,0:T(8,128)(2,1)S(1)}, u32[]{:S(2)}, u32[]{:S(2)}) collective-permute-start(bf16[2,2,128,128]{3,2,1,0:T(8,128)(2,1)S(1)} %copy.47), channel_id=1, source_target_pairs={{4,0},{8,4},{12,8},{16,12},{20,16},{24,20},{28,24},{5,1},{9,5},{13... | collective-permute-start | bytes 393224 | tf_op jit(solution)/shard_map/ppermute | solution.py:18
  93.1 2.0 %collective-permute-done.10 = bf16[2,2,128,128]{3,2,1,0:T(8,128)(2,1)S(1)} collective-permute-done((bf16[2,2,128,128]{3,2,1,0:T(8,128)(2,1)S(1)}, bf16[2,2,128,128]{3,2,1,0:T(8,128)(2,1)S(1)}, u32[]{:S(2)}, u32[]{:S(2)}) %collective-permute-start.10) | collective-permute-done | bytes 131104 | tf_op jit(solution)/shard_map/ppermute | solution.py:17
  95.2 2.8 %collective-permute-done.11 = bf16[2,2,128,128]{3,2,1,0:T(8,128)(2,1)S(1)} collective-permute-done((bf16[2,2,128,128]{3,2,1,0:T(8,128)(2,1)S(1)}, bf16[2,2,128,128]{3,2,1,0:T(8,128)(2,1)S(1)}, u32[]{:S(2)}, u32[]{:S(2)}) %collective-permute-start.11) | collective-permute-done | bytes 131104 | tf_op jit(solution)/shard_map/ppermute | solution.py:18
  98.0 2.3 %collective-permute-start.13 = (bf16[2,6,128,128]{3,2,1,0:T(8,128)(2,1)S(1)}, bf16[2,6,128,128]{3,2,1,0:T(8,128)(2,1)S(1)}, u32[]{:S(2)}, u32[]{:S(2)}) collective-permute-start(bf16[2,6,128,128]{3,2,1,0:T(8,128)(2,1)S(1)} %constant_dynamic-update-slice_fusion.3), channel_id=1, source_target_pairs={{1,0},{2,1},{3,2},{5,4},{6,5},{7,6},{9,8},{10,9},{11,10},{13,12},{... | collective-permute-start | bytes 1179656 | tf_op jit(solution)/shard_map/ppermute | solution.py:18
  100.3 3.3 %collective-permute-start.12 = (bf16[2,6,128,128]{3,2,1,0:T(8,128)(2,1)S(1)}, bf16[2,6,128,128]{3,2,1,0:T(8,128)(2,1)S(1)}, u32[]{:S(2)}, u32[]{:S(2)}) collective-permute-start(bf16[2,6,128,128]{3,2,1,0:T(8,128)(2,1)S(1)} %constant_dynamic-update-slice_fusion.3), channel_id=1, source_target_pairs={{0,1},{1,2},{2,3},{4,5},{5,6},{6,7},{8,9},{9,10},{10,11},{12,13},{... | collective-permute-start | bytes 1179656 | tf_op jit(solution)/shard_map/ppermute | solution.py:17
  103.5 3.5 %collective-permute-done.13 = bf16[2,6,128,128]{3,2,1,0:T(8,128)(2,1)S(1)} collective-permute-done((bf16[2,6,128,128]{3,2,1,0:T(8,128)(2,1)S(1)}, bf16[2,6,128,128]{3,2,1,0:T(8,128)(2,1)S(1)}, u32[]{:S(2)}, u32[]{:S(2)}) %collective-permute-start.13) | collective-permute-done | bytes 393248 | tf_op jit(solution)/shard_map/ppermute | solution.py:18
  111.8 8.4 %all_gather.18 = bf16[8,256,128]{2,1,0:T(8,128)(2,1)S(1)} all-gather(bf16[2,256,128]{2,1,0:T(8,128)(2,1)S(1)} %fusion.18), channel_id=1, replica_groups=mesh['horiz'=8,'vert'=4] {'vert'}, dimensions={0}, use_global_device_ids=true | all-gather | bytes 655360 | tf_op jit(solution)/shard_map/all_gather | solution.py:74
  121.5 2.5 %collective-permute-start.14 = (bf16[256,128]{1,0:T(8,128)(2,1)S(1)}, bf16[256,128]{1,0:T(8,128)(2,1)S(1)}, u32[]{:S(2)}, u32[]{:S(2)}) collective-permute-start(bf16[256,128]{1,0:T(8,128)(2,1)S(1)} %bitcast.92), channel_id=1, source_target_pairs={{0,1},{1,2},{2,3},{4,5},{5,6},{6,7},{8,9},{9,10},{10,11},{12,13},{... | collective-permute-start | bytes 196616 | tf_op jit(solution)/shard_map/ppermute | solution.py:26
  127.7 4.3 %collective-permute-start.16 = (bf16[2,2,128,128]{3,2,1,0:T(8,128)(2,1)S(1)}, bf16[2,2,128,128]{3,2,1,0:T(8,128)(2,1)S(1)}, u32[]{:S(2)}, u32[]{:S(2)}) collective-permute-start(bf16[2,2,128,128]{3,2,1,0:T(8,128)(2,1)S(1)} %copy.51), channel_id=1, source_target_pairs={{4,0},{8,4},{12,8},{16,12},{20,16},{24,20},{28,24},{5,1},{9,5},{13... | collective-permute-start | bytes 393224 | tf_op jit(solution)/shard_map/ppermute | solution.py:18
  132.0 2.0 %collective-permute-done.15 = bf16[2,2,128,128]{3,2,1,0:T(8,128)(2,1)S(1)} collective-permute-done((bf16[2,2,128,128]{3,2,1,0:T(8,128)(2,1)S(1)}, bf16[2,2,128,128]{3,2,1,0:T(8,128)(2,1)S(1)}, u32[]{:S(2)}, u32[]{:S(2)}) %collective-permute-start.15) | collective-permute-done | bytes 131104 | tf_op jit(solution)/shard_map/ppermute | solution.py:17
  134.1 2.8 %collective-permute-done.16 = bf16[2,2,128,128]{3,2,1,0:T(8,128)(2,1)S(1)} collective-permute-done((bf16[2,2,128,128]{3,2,1,0:T(8,128)(2,1)S(1)}, bf16[2,2,128,128]{3,2,1,0:T(8,128)(2,1)S(1)}, u32[]{:S(2)}, u32[]{:S(2)}) %collective-permute-start.16) | collective-permute-done | bytes 131104 | tf_op jit(solution)/shard_map/ppermute | solution.py:18
  136.9 2.3 %collective-permute-start.18 = (bf16[2,6,128,128]{3,2,1,0:T(8,128)(2,1)S(1)}, bf16[2,6,128,128]{3,2,1,0:T(8,128)(2,1)S(1)}, u32[]{:S(2)}, u32[]{:S(2)}) collective-permute-start(bf16[2,6,128,128]{3,2,1,0:T(8,128)(2,1)S(1)} %constant_dynamic-update-slice_fusion.6), channel_id=1, source_target_pairs={{1,0},{2,1},{3,2},{5,4},{6,5},{7,6},{9,8},{10,9},{11,10},{13,12},{... | collective-permute-start | bytes 1179656 | tf_op jit(solution)/shard_map/ppermute | solution.py:18
  139.2 3.4 %collective-permute-start.17 = (bf16[2,6,128,128]{3,2,1,0:T(8,128)(2,1)S(1)}, bf16[2,6,128,128]{3,2,1,0:T(8,128)(2,1)S(1)}, u32[]{:S(2)}, u32[]{:S(2)}) collective-permute-start(bf16[2,6,128,128]{3,2,1,0:T(8,128)(2,1)S(1)} %constant_dynamic-update-slice_fusion.6), channel_id=1, source_target_pairs={{0,1},{1,2},{2,3},{4,5},{5,6},{6,7},{8,9},{9,10},{10,11},{12,13},{... | collective-permute-start | bytes 1179656 | tf_op jit(solution)/shard_map/ppermute | solution.py:17
  142.6 3.3 %collective-permute-done.18 = bf16[2,6,128,128]{3,2,1,0:T(8,128)(2,1)S(1)} collective-permute-done((bf16[2,6,128,128]{3,2,1,0:T(8,128)(2,1)S(1)}, bf16[2,6,128,128]{3,2,1,0:T(8,128)(2,1)S(1)}, u32[]{:S(2)}, u32[]{:S(2)}) %collective-permute-start.18) | collective-permute-done | bytes 393248 | tf_op jit(solution)/shard_map/ppermute | solution.py:18
  150.7 8.4 %all_gather.19 = bf16[8,256,128]{2,1,0:T(8,128)(2,1)S(1)} all-gather(bf16[2,256,128]{2,1,0:T(8,128)(2,1)S(1)} %fusion.19), channel_id=1, replica_groups=mesh['horiz'=8,'vert'=4] {'vert'}, dimensions={0}, use_global_device_ids=true | all-gather | bytes 655360 | tf_op jit(solution)/shard_map/all_gather | solution.py:74
  160.4 2.5 %collective-permute-start.19 = (bf16[256,128]{1,0:T(8,128)(2,1)S(1)}, bf16[256,128]{1,0:T(8,128)(2,1)S(1)}, u32[]{:S(2)}, u32[]{:S(2)}) collective-permute-start(bf16[256,128]{1,0:T(8,128)(2,1)S(1)} %bitcast.93), channel_id=1, source_target_pairs={{0,1},{1,2},{2,3},{4,5},{5,6},{6,7},{8,9},{9,10},{10,11},{12,13},{... | collective-permute-start | bytes 196616 | tf_op jit(solution)/shard_map/ppermute | solution.py:26
  (89 shorter events, 41.2 us)
Async XLA Ops:
  0.0 32.2 %copy-start = (bf16[2,2,7,128,128]{4,3,2,1,0:T(8,128)(2,1)S(1)}, bf16[2,2,7,128,128]{4,3,2,1,0:T(8,128)(2,1)}, u32[]{:S(2)}) copy-start(bf16[2,2,7,128,128]{4,3,2,1,0:T(8,128)(2,1)} %param.9) | copy-start | bytes 2752516
  0.0 19.2 %copy-start.1 = (bf16[2,256,128]{2,1,0:T(8,128)(2,1)S(1)}, bf16[2,256,128]{2,1,0:T(8,128)(2,1)}, u32[]{:S(2)}) copy-start(bf16[2,256,128]{2,1,0:T(8,128)(2,1)} %param.8) | copy-start | bytes 393220
  0.0 19.1 %collective-permute-start.1 = (bf16[2,2,128,128]{3,2,1,0:T(8,128)(2,1)}, bf16[2,2,128,128]{3,2,1,0:T(8,128)(2,1)S(1)}, u32[]{:S(2)}, u32[]{:S(2)}) collective-permute-start(bf16[2,2,128,128]{3,2,1,0:T(8,128)(2,1)} %bitcast.82), channel_id=1, source_target_pairs={{4,0},{8,4},{12,8},{16,12},{20,16},{24,20},{28,24},{5,1},{9,5},{13... | collective-permute-start | bytes 393224 | tf_op jit(solution)/shard_map/ppermute | solution.py:18
  3.2 16.0 %collective-permute-start = (bf16[2,2,128,128]{3,2,1,0:T(8,128)(2,1)}, bf16[2,2,128,128]{3,2,1,0:T(8,128)(2,1)S(1)}, u32[]{:S(2)}, u32[]{:S(2)}) collective-permute-start(bf16[2,2,128,128]{3,2,1,0:T(8,128)(2,1)} %bitcast.83), channel_id=1, source_target_pairs={{0,4},{4,8},{8,12},{12,16},{16,20},{20,24},{24,28},{1,5},{5,9},{9,... | collective-permute-start | bytes 393224 | tf_op jit(solution)/shard_map/ppermute | solution.py:17
  7.1 17.7 %copy-start.5 = (s32[2,2]{1,0:T(2,128)S(1)}, s32[2,2]{1,0:T(2,128)}, u32[]{:S(2)}) copy-start(s32[2,2]{1,0:T(2,128)} %param.11) | copy-start | bytes 52
  7.1 17.8 %copy-start.4 = (s32[2,256]{1,0:T(2,128)S(1)}, s32[2,256]{1,0:T(2,128)}, u32[]{:S(2)}) copy-start(s32[2,256]{1,0:T(2,128)} %param.15) | copy-start | bytes 6148
  19.2 9.2 %copy-start.2 = (bf16[2,2,128,128]{3,2,1,0:T(8,128)(2,1)}, bf16[2,2,128,128]{3,2,1,0:T(8,128)(2,1)S(1)}, u32[]{:S(2)}) copy-start(bf16[2,2,128,128]{3,2,1,0:T(8,128)(2,1)S(1)} %collective-permute-done) | copy-start | bytes 393220
  19.2 9.1 %collective-permute-start.3 = (bf16[2,6,128,128]{3,2,1,0:T(8,128)(2,1)S(1)}, bf16[2,6,128,128]{3,2,1,0:T(8,128)(2,1)S(1)}, u32[]{:S(2)}, u32[]{:S(2)}) collective-permute-start(bf16[2,6,128,128]{3,2,1,0:T(8,128)(2,1)S(1)} %pad_maximum_fusion.4), channel_id=1, source_target_pairs={{1,0},{2,1},{3,2},{5,4},{6,5},{7,6},{9,8},{10,9},{11,10},{13,12},{... | collective-permute-start | bytes 1179656 | tf_op jit(solution)/shard_map/ppermute | solution.py:18
  21.3 8.2 %collective-permute-start.2 = (bf16[2,6,128,128]{3,2,1,0:T(8,128)(2,1)S(1)}, bf16[2,6,128,128]{3,2,1,0:T(8,128)(2,1)S(1)}, u32[]{:S(2)}, u32[]{:S(2)}) collective-permute-start(bf16[2,6,128,128]{3,2,1,0:T(8,128)(2,1)S(1)} %pad_maximum_fusion.4), channel_id=1, source_target_pairs={{0,1},{1,2},{2,3},{4,5},{5,6},{6,7},{8,9},{9,10},{10,11},{12,13},{... | collective-permute-start | bytes 1179656 | tf_op jit(solution)/shard_map/ppermute | solution.py:17
  33.9 12.3 %copy-start.3 = (f32[128]{0:T(128)S(1)}, f32[128]{0:T(128)}, u32[]{:S(2)}) copy-start(f32[128]{0:T(128)} %param.14) | copy-start | bytes 1540
  43.7 3.8 %collective-permute-start.4 = (bf16[256,128]{1,0:T(8,128)(2,1)S(1)}, bf16[256,128]{1,0:T(8,128)(2,1)S(1)}, u32[]{:S(2)}, u32[]{:S(2)}) collective-permute-start(bf16[256,128]{1,0:T(8,128)(2,1)S(1)} %bitcast.90), channel_id=1, source_target_pairs={{0,1},{1,2},{2,3},{4,5},{5,6},{6,7},{8,9},{9,10},{10,11},{12,13},{... | collective-permute-start | bytes 196616 | tf_op jit(solution)/shard_map/ppermute | solution.py:26
  48.0 8.2 %collective-permute-start.5 = (bf16[2,2,128,128]{3,2,1,0:T(8,128)(2,1)S(1)}, bf16[2,2,128,128]{3,2,1,0:T(8,128)(2,1)S(1)}, u32[]{:S(2)}, u32[]{:S(2)}) collective-permute-start(bf16[2,2,128,128]{3,2,1,0:T(8,128)(2,1)S(1)} %copy.42), channel_id=1, source_target_pairs={{0,4},{4,8},{8,12},{12,16},{16,20},{20,24},{24,28},{1,5},{5,9},{9,... | collective-permute-start | bytes 393224 | tf_op jit(solution)/shard_map/ppermute | solution.py:17
  49.9 9.1 %collective-permute-start.6 = (bf16[2,2,128,128]{3,2,1,0:T(8,128)(2,1)S(1)}, bf16[2,2,128,128]{3,2,1,0:T(8,128)(2,1)S(1)}, u32[]{:S(2)}, u32[]{:S(2)}) collective-permute-start(bf16[2,2,128,128]{3,2,1,0:T(8,128)(2,1)S(1)} %copy.42), channel_id=1, source_target_pairs={{4,0},{8,4},{12,8},{16,12},{20,16},{24,20},{28,24},{5,1},{9,5},{13... | collective-permute-start | bytes 393224 | tf_op jit(solution)/shard_map/ppermute | solution.py:18
  59.1 9.1 %collective-permute-start.8 = (bf16[2,6,128,128]{3,2,1,0:T(8,128)(2,1)S(1)}, bf16[2,6,128,128]{3,2,1,0:T(8,128)(2,1)S(1)}, u32[]{:S(2)}, u32[]{:S(2)}) collective-permute-start(bf16[2,6,128,128]{3,2,1,0:T(8,128)(2,1)S(1)} %constant_dynamic-update-slice_fusion), channel_id=1, source_target_pairs={{1,0},{2,1},{3,2},{5,4},{6,5},{7,6},{9,8},{10,9},{11,10},{13,12},{... | collective-permute-start | bytes 1179656 | tf_op jit(solution)/shard_map/ppermute | solution.py:18
  61.4 8.0 %collective-permute-start.7 = (bf16[2,6,128,128]{3,2,1,0:T(8,128)(2,1)S(1)}, bf16[2,6,128,128]{3,2,1,0:T(8,128)(2,1)S(1)}, u32[]{:S(2)}, u32[]{:S(2)}) collective-permute-start(bf16[2,6,128,128]{3,2,1,0:T(8,128)(2,1)S(1)} %constant_dynamic-update-slice_fusion), channel_id=1, source_target_pairs={{0,1},{1,2},{2,3},{4,5},{5,6},{6,7},{8,9},{9,10},{10,11},{12,13},{... | collective-permute-start | bytes 1179656 | tf_op jit(solution)/shard_map/ppermute | solution.py:17
  82.6 3.8 %collective-permute-start.9 = (bf16[256,128]{1,0:T(8,128)(2,1)S(1)}, bf16[256,128]{1,0:T(8,128)(2,1)S(1)}, u32[]{:S(2)}, u32[]{:S(2)}) collective-permute-start(bf16[256,128]{1,0:T(8,128)(2,1)S(1)} %bitcast.91), channel_id=1, source_target_pairs={{0,1},{1,2},{2,3},{4,5},{5,6},{6,7},{8,9},{9,10},{10,11},{12,13},{... | collective-permute-start | bytes 196616 | tf_op jit(solution)/shard_map/ppermute | solution.py:26
  86.9 8.2 %collective-permute-start.10 = (bf16[2,2,128,128]{3,2,1,0:T(8,128)(2,1)S(1)}, bf16[2,2,128,128]{3,2,1,0:T(8,128)(2,1)S(1)}, u32[]{:S(2)}, u32[]{:S(2)}) collective-permute-start(bf16[2,2,128,128]{3,2,1,0:T(8,128)(2,1)S(1)} %copy.47), channel_id=1, source_target_pairs={{0,4},{4,8},{8,12},{12,16},{16,20},{20,24},{24,28},{1,5},{5,9},{9,... | collective-permute-start | bytes 393224 | tf_op jit(solution)/shard_map/ppermute | solution.py:17
  88.8 9.1 %collective-permute-start.11 = (bf16[2,2,128,128]{3,2,1,0:T(8,128)(2,1)S(1)}, bf16[2,2,128,128]{3,2,1,0:T(8,128)(2,1)S(1)}, u32[]{:S(2)}, u32[]{:S(2)}) collective-permute-start(bf16[2,2,128,128]{3,2,1,0:T(8,128)(2,1)S(1)} %copy.47), channel_id=1, source_target_pairs={{4,0},{8,4},{12,8},{16,12},{20,16},{24,20},{28,24},{5,1},{9,5},{13... | collective-permute-start | bytes 393224 | tf_op jit(solution)/shard_map/ppermute | solution.py:18
  98.0 9.1 %collective-permute-start.13 = (bf16[2,6,128,128]{3,2,1,0:T(8,128)(2,1)S(1)}, bf16[2,6,128,128]{3,2,1,0:T(8,128)(2,1)S(1)}, u32[]{:S(2)}, u32[]{:S(2)}) collective-permute-start(bf16[2,6,128,128]{3,2,1,0:T(8,128)(2,1)S(1)} %constant_dynamic-update-slice_fusion.3), channel_id=1, source_target_pairs={{1,0},{2,1},{3,2},{5,4},{6,5},{7,6},{9,8},{10,9},{11,10},{13,12},{... | collective-permute-start | bytes 1179656 | tf_op jit(solution)/shard_map/ppermute | solution.py:18
  100.3 8.0 %collective-permute-start.12 = (bf16[2,6,128,128]{3,2,1,0:T(8,128)(2,1)S(1)}, bf16[2,6,128,128]{3,2,1,0:T(8,128)(2,1)S(1)}, u32[]{:S(2)}, u32[]{:S(2)}) collective-permute-start(bf16[2,6,128,128]{3,2,1,0:T(8,128)(2,1)S(1)} %constant_dynamic-update-slice_fusion.3), channel_id=1, source_target_pairs={{0,1},{1,2},{2,3},{4,5},{5,6},{6,7},{8,9},{9,10},{10,11},{12,13},{... | collective-permute-start | bytes 1179656 | tf_op jit(solution)/shard_map/ppermute | solution.py:17
  121.5 3.8 %collective-permute-start.14 = (bf16[256,128]{1,0:T(8,128)(2,1)S(1)}, bf16[256,128]{1,0:T(8,128)(2,1)S(1)}, u32[]{:S(2)}, u32[]{:S(2)}) collective-permute-start(bf16[256,128]{1,0:T(8,128)(2,1)S(1)} %bitcast.92), channel_id=1, source_target_pairs={{0,1},{1,2},{2,3},{4,5},{5,6},{6,7},{8,9},{9,10},{10,11},{12,13},{... | collective-permute-start | bytes 196616 | tf_op jit(solution)/shard_map/ppermute | solution.py:26
  125.8 8.2 %collective-permute-start.15 = (bf16[2,2,128,128]{3,2,1,0:T(8,128)(2,1)S(1)}, bf16[2,2,128,128]{3,2,1,0:T(8,128)(2,1)S(1)}, u32[]{:S(2)}, u32[]{:S(2)}) collective-permute-start(bf16[2,2,128,128]{3,2,1,0:T(8,128)(2,1)S(1)} %copy.51), channel_id=1, source_target_pairs={{0,4},{4,8},{8,12},{12,16},{16,20},{20,24},{24,28},{1,5},{5,9},{9,... | collective-permute-start | bytes 393224 | tf_op jit(solution)/shard_map/ppermute | solution.py:17
  127.7 9.1 %collective-permute-start.16 = (bf16[2,2,128,128]{3,2,1,0:T(8,128)(2,1)S(1)}, bf16[2,2,128,128]{3,2,1,0:T(8,128)(2,1)S(1)}, u32[]{:S(2)}, u32[]{:S(2)}) collective-permute-start(bf16[2,2,128,128]{3,2,1,0:T(8,128)(2,1)S(1)} %copy.51), channel_id=1, source_target_pairs={{4,0},{8,4},{12,8},{16,12},{20,16},{24,20},{28,24},{5,1},{9,5},{13... | collective-permute-start | bytes 393224 | tf_op jit(solution)/shard_map/ppermute | solution.py:18
  136.9 9.1 %collective-permute-start.18 = (bf16[2,6,128,128]{3,2,1,0:T(8,128)(2,1)S(1)}, bf16[2,6,128,128]{3,2,1,0:T(8,128)(2,1)S(1)}, u32[]{:S(2)}, u32[]{:S(2)}) collective-permute-start(bf16[2,6,128,128]{3,2,1,0:T(8,128)(2,1)S(1)} %constant_dynamic-update-slice_fusion.6), channel_id=1, source_target_pairs={{1,0},{2,1},{3,2},{5,4},{6,5},{7,6},{9,8},{10,9},{11,10},{13,12},{... | collective-permute-start | bytes 1179656 | tf_op jit(solution)/shard_map/ppermute | solution.py:18
  139.2 8.0 %collective-permute-start.17 = (bf16[2,6,128,128]{3,2,1,0:T(8,128)(2,1)S(1)}, bf16[2,6,128,128]{3,2,1,0:T(8,128)(2,1)S(1)}, u32[]{:S(2)}, u32[]{:S(2)}) collective-permute-start(bf16[2,6,128,128]{3,2,1,0:T(8,128)(2,1)S(1)} %constant_dynamic-update-slice_fusion.6), channel_id=1, source_target_pairs={{0,1},{1,2},{2,3},{4,5},{5,6},{6,7},{8,9},{9,10},{10,11},{12,13},{... | collective-permute-start | bytes 1179656 | tf_op jit(solution)/shard_map/ppermute | solution.py:17
  160.4 3.8 %collective-permute-start.19 = (bf16[256,128]{1,0:T(8,128)(2,1)S(1)}, bf16[256,128]{1,0:T(8,128)(2,1)S(1)}, u32[]{:S(2)}, u32[]{:S(2)}) collective-permute-start(bf16[256,128]{1,0:T(8,128)(2,1)S(1)} %bitcast.93), channel_id=1, source_target_pairs={{0,1},{1,2},{2,3},{4,5},{5,6},{6,7},{8,9},{9,10},{10,11},{12,13},{... | collective-permute-start | bytes 196616 | tf_op jit(solution)/shard_map/ppermute | solution.py:26
where the time goes:
time: 169 us; the launch traced here: 165 us
  starting transfers between devices  56.4 us (33%)
  blocking collectives  44.7 us (26%)
  waiting for transfers between devices  37.6 us (22%)
  matrix products  11.4 us (7%)
  local copies, waits for them, and re-layouts  9.57 us (6%)
  other arithmetic  5.1 us (3%)
    all_gather x4, blocking collectives, on_device(): lax.all_gather(loaded, 'vert', axis=0, tiled=True).astype(jnp.float32)  33.6 us
    ppermute x8, starting transfers between devices, extended(): after = lax.ppermute(leading, axis, down)  24.9 us
    ppermute x8, waiting for transfers between devices, extended(): after = lax.ppermute(leading, axis, down)  22.1 us
    ppermute x8, starting transfers between devices, extended(): before = lax.ppermute(last, axis, up)  21.5 us
    all_gather x1, blocking collectives, on_device(): all_columns = lax.all_gather(implicit_columns, 'vert', axis=0, tiled=True)  11.1 us
    ppermute x8, waiting for transfers between devices, extended(): before = lax.ppermute(last, axis, up)  10.8 us
    ppermute x4, starting transfers between devices, from_behind(): lax.ppermute(value, axis, [(source, source + steps) for source in range(l...  10 us
    dot_general x4, matrix products, on_device(): jnp.einsum('ltjab,ltjbs->ltas', explicit_tiles, picked, preferred_element...  6.59 us
  transfers between devices with their start and end apart: 20, of which 18 were waited for; matrix products, arithmetic and copies ran while one was open for 2% of the time, Pallas kernels for 0%

commit v1 on v0

v1 whole, which is shorter than its diff:
```python
import functools

import jax
import jax.numpy as jnp
from jax import lax
from jax.experimental import pallas as pl
from jax.experimental.pallas import tpu as pltpu
from jax.sharding import PartitionSpec as P

REACH = 2
STEPS = 4
Q = 2
MESH = pl.DeviceIdType.MESH
F32 = jnp.float32
BF16 = jnp.bfloat16


def kernel(
    h_size,
    v_size,
    tracer,
    tiles,
    source,
    extra,
    settling,
    columns,
    counts,
    out,
    weights,
    gath,
    other,
    src_t,
    fall,
    ops,
    a_win,
    w_win,
    pos,
    send_sem,
    recv_sem,
    ops_send,
    ops_recv,
    *halos,
):
    lev_dev, cells_dev, classes = tracer.shape
    slots, size = tiles.shape[2], tiles.shape[3]
    tiles_dev = cells_dev // size
    window = lev_dev + 2 * REACH
    levels = lev_dev * v_size
    h_tiles = h_size * tiles_dev
    ch = classes // Q
    h = lax.axis_index("horiz")
    v = lax.axis_index("vert")
    even = lax.rem(h, 2) == 0
    core = lax.rem(v, 2)
    base = 2 * (v // 2)
    partner = jnp.where(even, h + 1, h - 1)
    ahead = jnp.where(even, h + 2, h - 2)
    behind = jnp.where(even, h - 2, h + 2)
    has_ahead = (ahead >= 0) & (ahead < h_size)
    has_behind = (behind >= 0) & (behind < h_size)

    def vert(d):
        flipped = v
        if d & 1:
            flipped = flipped + 1 - 2 * core
        if d & 2:
            flipped = lax.rem(flipped + 2, 4)
        return {"horiz": h, "vert": flipped}

    near = {"horiz": partner, "vert": v}
    front = {"horiz": ahead, "vert": v}
    back = {"horiz": behind, "vert": v}

    barrier = pltpu.get_barrier_semaphore()
    for d in (1, 2, 3):
        pl.semaphore_signal(barrier, inc=1, device_id=vert(d), device_id_type=MESH)
    pl.semaphore_signal(barrier, inc=1, device_id=near, device_id_type=MESH)

    @pl.when(has_ahead)
    def _():
        pl.semaphore_signal(barrier, inc=1, device_id=front, device_id_type=MESH)

    @pl.when(has_behind)
    def _():
        pl.semaphore_signal(barrier, inc=1, device_id=back, device_id_type=MESH)

    own_t = 2 + core
    near_t = jnp.where(even, 4, 0) + core
    far_t = jnp.where(even, 0, 4) + core

    def remote(src, dst, p, q, kind, where):
        return pltpu.make_async_remote_copy(
            src_ref=src,
            dst_ref=dst,
            send_sem=send_sem.at[p, q, kind],
            recv_sem=recv_sem.at[p, q, kind],
            device_id=where,
            device_id_type=MESH,
        )

    def x_copies(p, q):
        par = p % 2
        here = gath.at[par, q, pl.ds(lev_dev * v, lev_dev)]
        return [
            remote(here if d == 2 else other.at[par, q], here, p, q, d - 1, vert(d))
            for d in (2, 3, 1)
        ]

    def block(p, q, where):
        return halos[p % 2 * Q + q].at[pl.ds(where * window, window)]

    def near_copy(p, q):
        return remote(block(p, q, own_t), block(p, q, far_t), p, q, 3, near)

    def side_own(p, q):
        return remote(block(p, q, own_t), block(p, q, own_t), p, q, 4, vert(1))

    def front_copy(p, q):
        return remote(block(p, q, near_t), block(p, q, far_t), p, q, 5, front)

    def side_near(p, q):
        return remote(block(p, q, near_t), block(p, q, near_t), p, q, 6, vert(1))

    def side_far(p, q):
        return remote(block(p, q, far_t), block(p, q, far_t), p, q, 7, vert(1))

    def put(p, q, on_core, level, value):
        if on_core:
            gath[p % 2, q, lev_dev * v + level] = value
        else:
            other[p % 2, q, level] = value

    def load_first(q):
        for on_core in (False, True):
            t = core if on_core else 1 - core
            for level in range(lev_dev):
                tile = tracer[level, pl.ds(pl.multiple_of(t * size, size), size), :]
                value = tile.T[q * ch : (q + 1) * ch]
                put(0, q, on_core, level, value)

    def explicit(p, q):
        for on_core in (False, True):
            t = core if on_core else 1 - core
            for level in range(lev_dev):
                picked = jnp.concatenate(
                    [
                        halos[(p - 1) % 2 * Q + q][pos[level, t * slots + j]]
                        for j in range(slots)
                    ],
                    axis=1,
                )
                flow = jnp.dot(
                    picked, weights[level, t], preferred_element_type=F32
                )
                if level == 0:
                    flow = flow + src_t[t, q * ch : (q + 1) * ch, :]
                put(p, q, on_core, level, flow.astype(BF16))

    def stage_a(p, q):
        if p == 0:
            load_first(q)
        else:
            explicit(p, q)
        if p == 0 and q == 0:
            count = 4 + has_ahead.astype(jnp.int32) + has_behind.astype(jnp.int32)
            pl.semaphore_wait(barrier, count)
        for copy in x_copies(p, q):
            copy.start()

    def sends_done(p, q):
        for copy in x_copies(p, q):
            copy.wait_send()
        side_own(p, q).wait_send()
        if p == STEPS:
            return
        near_copy(p, q).wait_send()
        side_near(p, q).wait_send()

        @pl.when(has_ahead)
        def _():
            front_copy(p, q).wait_send()

        @pl.when(has_behind)
        def _():
            side_far(p, q).wait_send()

    def solve(p, q):
        par = p % 2
        halo = halos[par * Q + q]
        first = own_t * window
        if p == 0:
            for k in range(window):
                halo[first + k] = gath[par, q, base + k]
            return
        rows = 16

        def body(i, carry):
            at = pl.ds(pl.multiple_of(i * rows, rows), rows)
            loaded = [gath[par, q, m, at, :].astype(F32) for m in range(levels)]
            rate = fall[pl.ds(pl.multiple_of(q * ch + i * rows, rows), rows), :]
            stay = 1.0 - rate
            above = None
            for k in range(window + 1):
                a = a_win[k * levels : (k + 1) * levels, :]
                mixed = a[0:1] * loaded[0]
                for m in range(1, levels):
                    mixed = mixed + a[m : m + 1] * loaded[m]
                if k:
                    settled = stay * mixed + rate * above
                    wet = w_win[k - 1 : k, :]
                    halo[first + k - 1, at, :] = (wet * settled).astype(BF16)
                above = mixed
            return carry

        lax.fori_loop(0, ch // rows, body, 0)

    def stage_b(p, q):
        for copy in x_copies(p, q):
            copy.wait_recv()
        if p:
            sends_done(p - 1, q)
        solve(p, q)
        if p < STEPS:
            near_copy(p, q).start()
        side_own(p, q).start()

    def stage_c(p, q):
        near_copy(p, q).wait_recv()

        @pl.when(has_ahead)
        def _():
            front_copy(p, q).start()

        side_near(p, q).start()

    def stage_d(p, q):
        @pl.when(has_behind)
        def _():
            front_copy(p, q).wait_recv()
            side_far(p, q).start()

    def stage_e(p, q):
        side_own(p, q).wait_recv()
        side_near(p, q).wait_recv()

        @pl.when(has_behind)
        def _():
            side_far(p, q).wait_recv()

    def ops_copy(d):
        return pltpu.make_async_remote_copy(
            src_ref=extra,
            dst_ref=ops.at[v],
            send_sem=ops_send.at[d - 1],
            recv_sem=ops_recv.at[d - 1],
            device_id=vert(d),
            device_id_type=MESH,
        )

    def prepare():
        for level in range(lev_dev):
            for t in range(tiles_dev):
                for j in range(slots):
                    column = columns[level, t * slots + j]
                    row = lax.div(column, h_tiles) - base
                    across = lax.rem(column, h_tiles) - tiles_dev * h + REACH
                    last = 3 * tiles_dev * window - 1
                    pos[level, t * slots + j] = jnp.clip(across * window + row, 0, last)
                    live = (j < counts[level, t]).astype(F32)
                    weights[level, t, j * size : (j + 1) * size, :] = (
                        tiles[level, t, j].astype(F32).T * live
                    ).astype(BF16)
        on_top = (v == 0).astype(F32)
        for t in range(tiles_dev):
            src_t[t] = source[t * size : (t + 1) * size, :].astype(F32).T * on_top
        fall[...] = jnp.broadcast_to(settling[...], (size, classes)).T

    ops[v] = extra[...]
    for q in range(Q):
        stage_a(0, q)
    for d in (1, 2, 3):
        ops_copy(d).start()
    prepare()
    for q in range(Q):
        stage_b(0, q)
    for d in (1, 2, 3):
        ops_copy(d).wait()
    square = levels * levels
    for k in range(window + 1):
        level = base + k - 1
        row = pl.ds(pl.multiple_of(jnp.maximum(level, 0) * levels, levels), levels)
        keep = (level >= 0).astype(F32)
        a_win[k * levels : (k + 1) * levels, :] = keep * (
            ops[2 * core, row, :] + ops[2 * core + 1, row, :]
        )
        if k:
            w_win[k - 1 : k, :] = ops[
                level // lev_dev,
                pl.ds(square + lax.rem(level, lev_dev) * tiles_dev + core, 1),
                :,
            ]
    for p in range(STEPS):
        for q in range(Q):
            stage_c(p, q)
        for q in range(Q):
            stage_d(p, q)
        for q in range(Q):
            stage_e(p, q)
            stage_a(p + 1, q)
        for q in range(Q):
            stage_b(p + 1, q)
    for q in range(Q):
        side_own(STEPS, q).wait_recv()
    for level in range(lev_dev):
        for t in range(tiles_dev):
            where = (2 + t) * window + lev_dev * v - base + level
            whole = jnp.concatenate(
                [halos[STEPS % 2 * Q + q][where] for q in range(Q)], axis=0
            )
            out[level, t * size : (t + 1) * size, :] = whole.T
    for q in range(Q):
        sends_done(STEPS, q)


def on_device(h_size, v_size, tracer, tiles, columns, counts, source, implicit, settling, wet):
    lev_dev, cells_dev, classes = tracer.shape
    slots, size = tiles.shape[2], tiles.shape[3]
    tiles_dev = cells_dev // size
    levels = implicit.shape[1]
    share = implicit.shape[0]
    window = lev_dev + 2 * REACH
    assert lev_dev == 2 and tiles_dev == 2 and v_size == 4 and h_size % 2 == 0
    ch = classes // Q
    flat = implicit.reshape(share, levels * levels).T
    right = lax.rem(lax.axis_index("vert"), 2).astype(F32)
    flat = jnp.concatenate([flat * (1.0 - right), flat * right], axis=1)
    wet_rows = wet.astype(F32).reshape(lev_dev * tiles_dev, size)
    extra = jnp.concatenate([flat, wet_rows, jnp.zeros_like(wet_rows)], axis=0)
    vm = pl.BlockSpec(memory_space=pltpu.VMEM)
    sm = pl.BlockSpec(memory_space=pltpu.SMEM)
    phases = STEPS + 1
    return pl.pallas_call(
        functools.partial(kernel, h_size, v_size),
        out_shape=jax.ShapeDtypeStruct(tracer.shape, tracer.dtype),
        in_specs=[vm] * 5 + [sm] * 2,
        out_specs=vm,
        scratch_shapes=[
            pltpu.VMEM((lev_dev, tiles_dev, slots * size, size), BF16),
            pltpu.VMEM((2, Q, levels, ch, size), BF16),
            pltpu.VMEM((2, Q, lev_dev, ch, size), BF16),
            pltpu.VMEM((tiles_dev, classes, size), F32),
            pltpu.VMEM((classes, size), F32),
            pltpu.VMEM((v_size,) + extra.shape, F32),
            pltpu.VMEM(((window + 1) * levels, size), F32),
            pltpu.VMEM((8, size), F32),
            pltpu.SMEM((lev_dev, tiles_dev * slots), jnp.int32),
            pltpu.SemaphoreType.DMA((phases, Q, 8)),
            pltpu.SemaphoreType.DMA((phases, Q, 8)),
            pltpu.SemaphoreType.DMA((3,)),
            pltpu.SemaphoreType.DMA((3,)),
        ]
        + [pltpu.VMEM((3 * tiles_dev * window, ch, size), BF16)] * (2 * Q),
        compiler_params=pltpu.CompilerParams(
            collective_id=0, has_side_effects=True, vmem_limit_bytes=32 * 2**20
        ),
    )(
        tracer,
        tiles,
        source,
        extra,
        settling.reshape(1, classes),
        columns.reshape(lev_dev, tiles_dev * slots),
        counts,
    )


def solution(mesh):
    placed = (
        P("vert", "horiz", None),
        P("vert", "horiz", None, None, None),
        P("vert", "horiz", None),
        P("vert", "horiz"),
        P("horiz", None),
        P(("horiz", "vert"), None, None),
        P(),
        P("vert", "horiz"),
    )
    body = functools.partial(on_device, mesh.shape["horiz"], mesh.shape["vert"])
    return jax.shard_map(
        body, mesh=mesh, in_specs=placed, out_specs=P("vert", "horiz", None), check_vma=False
    )
```

time: 169 us -> 71.4 us (0.42); the launches traced: 165 us -> 70.7 us
  Pallas kernels: 0 us -> 66.4 us
  starting transfers between devices: 56.4 us -> 0 us
  blocking collectives: 44.7 us -> 0 us
  waiting for transfers between devices: 37.6 us -> 0 us
  matrix products: 11.4 us -> 0 us
  local copies, waits for them, and re-layouts: 9.57 us -> 3.42 us
  other arithmetic: 5.1 us -> 0.77 us
    pallas_call x0 -> x1, Pallas kernels: none -> 66.4 us  [on_device(): pl.pallas_call(functools.partial(kernel, h_size, v_size), out_shape=jax.S...]
    ppermute x20 -> x0, starting transfers between devices: 56.4 us -> none  [the longest x8 24.9 us: extended(): after = lax.ppermute(leading, axis, down)]
    all_gather x5 -> x0, blocking collectives: 44.7 us -> none  [the longest x4 33.6 us: on_device(): lax.all_gather(loaded, 'vert', axis=0, tiled=True).astype(jnp.float32)]
    ppermute x20 -> x0, waiting for transfers between devices: 37.6 us -> none  [the longest x8 22.1 us: extended(): after = lax.ppermute(leading, axis, down)]
    dot_general x8 -> x0, matrix products: 11.4 us -> none  [the longest x4 6.59 us: on_device(): jnp.einsum('ltjab,ltjbs->ltas', explicit_tiles, picked, preferred_element...]
    gather x4 -> x0, local copies, waits for them, and re-layouts: 6.5 us -> none  [on_device(): picked = flattened[position] * live_slots[:, :, :, None, None]]
    convert_element_type x11 -> x1, other arithmetic: 2.87 us -> 0.68 us  [on_device(): wet_rows = wet.astype(F32).reshape(lev_dev * tiles_dev, size)]
  transfers between devices with their start and end apart: 20 -> 0, of which waited for: 18 -> 0; matrix products, arithmetic and copies ran while one was open for 2% -> 0% of each run, Pallas kernels for 0% -> 0%
where the time goes in v1:
time: 71.4 us; the launch traced here: 70.7 us
  Pallas kernels  66.4 us (93%)
  local copies, waits for them, and re-layouts  3.42 us (5%)
  other arithmetic  0.77 us (1%)
    pallas_call x1, Pallas kernels, on_device(): pl.pallas_call(functools.partial(kernel, h_size, v_size), out_shape=jax.S...  66.4 us
    unnamed x13, local copies, waits for them, and re-layouts  2.57 us

profile of v1, /device:TPU:25, one launch (start us, length us, event | category | flops | bytes accessed | tf_op | source)
XLA Modules:
  0.0 70.7 jit_solution(14199961053481705919)
XLA Ops:
  0.0 0.0 copy-start.5
  0.0 0.0 copy-start.1
  0.0 0.1 pad.3.clone
  0.1 0.8 %reshape.16.columns = s32[2,14]{1,0:T(2,128)S(1)} reshape(s32[2,2,7]{2,1,0:T(2,128)} %param.10) | data formatting | bytes 224 | tf_op jit(solution)/shard_map/reshape | solution.py:372
  0.8 0.7 convert_element_type.7
  1.5 0.0 copy-done.5
  1.6 0.0 copy-start.2
  1.6 0.0 copy-start.3
  1.6 0.0 copy-start.4
  1.6 0.1 maximum_maximum_fusion.extra
  1.7 0.0 copy-done.1
  1.7 0.7 copy-done.2
  2.4 0.0 copy-done.3
  2.4 0.0 copy-done.4
  2.4 0.0 copy-start
  2.4 1.2 %copy-done = bf16[2,2,7,128,128]{4,3,2,1,0:T(8,128)(2,1)S(1)} copy-done((bf16[2,2,7,128,128]{4,3,2,1,0:T(8,128)(2,1)S(1)}, bf16[2,2,7,128,128]{4,3,2,1,0:T(8,128)(2,1)}, u32[]{:S(2)}) %copy-start) | copy-done | bytes 917528
  3.6 66.4 %shard_map.82 = bf16[2,256,128]{2,1,0:T(8,128)(2,1)S(1)} custom-call(bf16[2,256,128]{2,1,0:T(8,128)(2,1)S(1)} %copy-done.1, bf16[2,2,7,128,128]{4,3,2,1,0:T(8,128)(2,1)S(1)} %copy-done, bf16[256,128]{1,0:T(8,128)(2,1)S(1)} %copy-done.2, f32[72,128]{1,0:T(8,128)S(1)} %maximum_maximum_fusion.extra, f32[1,128]{1,0:T(1,128)S(1)} %bitcast.9, ...), custom_call_target="tpu_custom_call" | custom-call | tf_op jit(solution)/shard_map/pallas_call | solution.py:342
  70.0 0.7 copy.10
  (3 shorter events, 0.0 us)
Async XLA Ops:
  0.0 1.5 %copy-start.5 = (f32[64,8,8]{0,2,1:T(8,128)S(1)}, f32[64,8,8]{0,2,1:T(8,128)}, u32[]{:S(2)}) copy-start(f32[64,8,8]{0,2,1:T(8,128)} %param.13) | copy-start | bytes 49156
  0.0 1.7 %copy-start.1 = (bf16[2,256,128]{2,1,0:T(8,128)(2,1)S(1)}, bf16[2,256,128]{2,1,0:T(8,128)(2,1)}, u32[]{:S(2)}) copy-start(bf16[2,256,128]{2,1,0:T(8,128)(2,1)} %tracer.1) | copy-start | bytes 393220
  1.6 0.8 %copy-start.2 = (bf16[256,128]{1,0:T(8,128)(2,1)S(1)}, bf16[256,128]{1,0:T(8,128)(2,1)}, u32[]{:S(2)}) copy-start(bf16[256,128]{1,0:T(8,128)(2,1)} %source.1) | copy-start | bytes 196612
  1.6 0.8 %copy-start.3 = (s32[2,2]{1,0:T(2,128)S(1)}, s32[2,2]{1,0:T(2,128)}, u32[]{:S(2)}) copy-start(s32[2,2]{1,0:T(2,128)} %counts.1) | copy-start | bytes 52
  1.6 0.8 %copy-start.4 = (f32[128]{0:T(128)S(1)}, f32[128]{0:T(128)}, u32[]{:S(2)}) copy-start(f32[128]{0:T(128)} %param.14) | copy-start | bytes 1540
  2.4 1.2 %copy-start = (bf16[2,2,7,128,128]{4,3,2,1,0:T(8,128)(2,1)S(1)}, bf16[2,2,7,128,128]{4,3,2,1,0:T(8,128)(2,1)}, u32[]{:S(2)}) copy-start(bf16[2,2,7,128,128]{4,3,2,1,0:T(8,128)(2,1)} %tiles.1) | copy-start | bytes 2752516

commit v2 on v1

v2 whole, which is shorter than its diff:
```python
import functools

import jax
import jax.numpy as jnp
from jax import lax
from jax.experimental import pallas as pl
from jax.experimental.pallas import tpu as pltpu
from jax.sharding import PartitionSpec as P

REACH = 2
STEPS = 4
Q = 4
MESH = pl.DeviceIdType.MESH
F32 = jnp.float32
BF16 = jnp.bfloat16


def kernel(
    h_size,
    v_size,
    tracer,
    tiles,
    source,
    extra,
    settling,
    columns,
    counts,
    out,
    weights,
    turned,
    gath,
    other,
    final,
    src_t,
    fall,
    ops,
    a_win,
    w_win,
    cols_v,
    cols_s,
    pos,
    send_sem,
    recv_sem,
    first_send,
    first_recv,
    last_send,
    last_recv,
    ops_send,
    ops_recv,
    pair_send,
    pair_recv,
    local_sem,
    *halos,
):
    lev_dev, cells_dev, classes = tracer.shape
    slots, size = tiles.shape[2], tiles.shape[3]
    tiles_dev = cells_dev // size
    window = lev_dev + 2 * REACH
    levels = lev_dev * v_size
    lev_chip = 2 * lev_dev
    h_tiles = h_size * tiles_dev
    half = classes // 2
    ch = half // Q
    blk = tiles_dev * window
    h = lax.axis_index("horiz")
    v = lax.axis_index("vert")
    even = lax.rem(h, 2) == 0
    core = lax.rem(v, 2)
    chip = v // 2
    base = 2 * chip
    partner = jnp.where(even, h + 1, h - 1)
    ahead = jnp.where(even, h + 2, h - 2)
    behind = jnp.where(even, h - 2, h + 2)
    has_ahead = (ahead >= 0) & (ahead < h_size)
    has_behind = (behind >= 0) & (behind < h_size)

    def vert(d):
        flipped = v
        if d & 1:
            flipped = flipped + 1 - 2 * core
        if d & 2:
            flipped = lax.rem(flipped + 2, 4)
        return {"horiz": h, "vert": flipped}

    near = {"horiz": partner, "vert": v}
    front = {"horiz": ahead, "vert": v}
    back = {"horiz": behind, "vert": v}

    barrier = pltpu.get_barrier_semaphore()
    for where in (vert(1), vert(2), vert(3), near):
        pl.semaphore_signal(barrier, inc=1, device_id=where, device_id_type=MESH)

    @pl.when(has_ahead)
    def _():
        pl.semaphore_signal(barrier, inc=1, device_id=front, device_id_type=MESH)

    @pl.when(has_behind)
    def _():
        pl.semaphore_signal(barrier, inc=1, device_id=back, device_id_type=MESH)

    near_at = jnp.where(even, 2 * blk, 0)
    far_at = jnp.where(even, 0, 2 * blk)

    def copy_to(src, dst, send, recv, where):
        return pltpu.make_async_remote_copy(
            src_ref=src,
            dst_ref=dst,
            send_sem=send,
            recv_sem=recv,
            device_id=where,
            device_id_type=MESH,
        )

    def remote(src, dst, p, q, kind, where):
        return copy_to(
            src, dst, send_sem.at[p, q, kind], recv_sem.at[p, q, kind], where
        )

    def x_copies(p, q):
        if p == 0:
            here = gath.at[0, q, pl.ds(lev_dev * v, lev_dev)]
            return [
                copy_to(
                    here if d == 2 else other.at[q],
                    here,
                    first_send.at[q, d - 1],
                    first_recv.at[q, d - 1],
                    vert(d),
                )
                for d in (2, 3, 1)
            ]
        here = gath.at[p % 2, q, pl.ds(lev_chip * chip, lev_chip)]
        return [remote(here, here, p, q, 0, vert(2))]

    def block(p, q, at):
        return halos[p % 2 * Q + q].at[pl.ds(at, blk)]

    def near_copy(p, q):
        return remote(block(p, q, blk), block(p, q, far_at), p, q, 1, near)

    def front_copy(p, q):
        return remote(block(p, q, near_at), block(p, q, far_at), p, q, 2, front)

    def last_copies(q):
        theirs = lev_dev * (v + 1 - 2 * core) - base
        halo = halos[STEPS % 2 * Q + q]
        return [
            copy_to(
                halo.at[pl.ds(blk + t * window + theirs, lev_dev)],
                final.at[core * Q + q, t],
                last_send.at[q, t],
                last_recv.at[q, t],
                vert(1),
            )
            for t in range(tiles_dev)
        ]

    def pair_copies():
        mine = weights.at[pl.ds(lev_dev * core, lev_dev)]
        cols = cols_v.at[core]
        return [
            copy_to(cols, cols, pair_send.at[0], pair_recv.at[0], vert(1)),
            copy_to(mine, mine, pair_send.at[1], pair_recv.at[1], vert(1)),
        ]

    def load_first(q):
        for level in range(lev_dev):
            for t in range(tiles_dev):
                ours = pl.ds(pl.multiple_of(core * half + q * ch, ch), ch)
                theirs = pl.ds(pl.multiple_of((1 - core) * half + q * ch, ch), ch)
                gath[0, q, lev_dev * v + level, t] = turned[level, t, ours, :]
                other[q, level, t] = turned[level, t, theirs, :]

    def explicit(p, q):
        for level in range(lev_chip):
            for t in range(tiles_dev):
                picked = jnp.concatenate(
                    [
                        halos[(p - 1) % 2 * Q + q][pos[level, t * slots + j]]
                        for j in range(slots)
                    ],
                    axis=1,
                )
                flow = jnp.dot(
                    picked, weights[level, t], preferred_element_type=F32
                )
                if level == 0:
                    ours = pl.ds(pl.multiple_of(core * half + q * ch, ch), ch)
                    flow = flow + src_t[t, ours, :]
                gath[p % 2, q, lev_chip * chip + level, t] = flow.astype(BF16)

    def stage_a(p, q):
        if p == 0:
            load_first(q)
        else:
            explicit(p, q)
        for copy in x_copies(p, q):
            copy.start()

    def sends_done(p, q):
        for copy in x_copies(p, q):
            copy.wait_send()
        if p == STEPS:
            return
        near_copy(p, q).wait_send()

        @pl.when(has_ahead)
        def _():
            front_copy(p, q).wait_send()

    def solve(p, q):
        par = p % 2
        halo = halos[par * Q + q]
        if p == 0:
            for t in range(tiles_dev):
                for k in range(window):
                    halo[blk + t * window + k] = gath[par, q, base + k, t]
            return
        rows = 16

        for t in range(tiles_dev):
            for i in range(ch // rows):
                at = slice(i * rows, (i + 1) * rows)
                loaded = [gath[par, q, m, t, at, :].astype(F32) for m in range(levels)]
                start = core * half + q * ch + i * rows
                rate = fall[pl.ds(pl.multiple_of(start, rows), rows), :]
                stay = 1.0 - rate
                above = None
                for k in range(window + 1):
                    mixed = None
                    for m in range(levels):
                        r = k * levels + m
                        term = a_win[t, r : r + 1, :] * loaded[m]
                        mixed = term if m == 0 else mixed + term
                    if k:
                        settled = stay * mixed + rate * above
                        wet = w_win[t, k - 1 : k, :]
                        halo[blk + t * window + k - 1, at, :] = (wet * settled).astype(BF16)
                    above = mixed

    def stage_b(p, q):
        for copy in x_copies(p, q):
            copy.wait_recv()
        if p:
            sends_done(p - 1, q)
        solve(p, q)
        if p < STEPS:
            near_copy(p, q).start()
        else:
            for copy in last_copies(q):
                copy.start()

    def stage_c(p, q):
        near_copy(p, q).wait_recv()

        @pl.when(has_ahead)
        def _():
            front_copy(p, q).start()

    def stage_d(p, q):
        @pl.when(has_behind)
        def _():
            front_copy(p, q).wait_recv()

    def ops_copy(d):
        return copy_to(
            extra, ops.at[v], ops_send.at[d - 1], ops_recv.at[d - 1], vert(d)
        )

    def prepare():
        for level in range(lev_dev):
            for t in range(tiles_dev):
                for j in range(slots):
                    live = (j < counts[level, t]).astype(F32)
                    weights[lev_dev * core + level, t, j * size : (j + 1) * size, :] = (
                        tiles[level, t, j].astype(F32).T * live
                    ).astype(BF16)

    def prepare_more():
        on_top = (chip == 0).astype(F32)
        for t in range(tiles_dev):
            src_t[t] = source[t * size : (t + 1) * size, :].astype(F32).T * on_top
        fall[...] = jnp.broadcast_to(settling[...], (size, classes)).T

    def positions():
        local = pltpu.make_async_copy(cols_v, cols_s, local_sem)
        local.start()
        local.wait()
        last = 3 * blk - 1
        for level in range(lev_chip):
            for n in range(tiles_dev * slots):
                column = cols_s[level // lev_dev, level % lev_dev, n]
                row = lax.div(column, h_tiles) - base
                across = lax.rem(column, h_tiles) - tiles_dev * h + REACH
                pos[level, n] = jnp.clip(across * window + row, 0, last)

    def operators():
        square = levels * levels
        for t in range(tiles_dev):
            for k in range(window + 1):
                level = base + k - 1
                row = pl.ds(
                    pl.multiple_of(jnp.maximum(level, 0) * levels, levels), levels
                )
                keep = (level >= 0).astype(F32)
                a_win[t, k * levels : (k + 1) * levels, :] = keep * (
                    ops[2 * t, row, :] + ops[2 * t + 1, row, :]
                )
                if k:
                    w_win[t, k - 1 : k, :] = ops[
                        level // lev_dev,
                        pl.ds(square + lax.rem(level, lev_dev) * tiles_dev + t, 1),
                        :,
                    ]

    ops[v] = extra[...]
    cols_v[core] = columns[...]
    for level in range(lev_dev):
        for t in range(tiles_dev):
            turned[level, t] = tracer[level, t * size : (t + 1) * size, :].T
    count = 4 + has_ahead.astype(jnp.int32) + has_behind.astype(jnp.int32)
    pl.semaphore_wait(barrier, count)
    for q in range(Q):
        stage_a(0, q)
    for d in (1, 2, 3):
        ops_copy(d).start()
    pair = pair_copies()
    pair[0].start()
    prepare()
    pair[1].start()
    for q in range(Q):
        stage_b(0, q)
    prepare_more()
    for d in (1, 2, 3):
        ops_copy(d).wait()
    operators()
    pair[0].wait()
    positions()
    for p in range(STEPS):
        for q in range(Q):
            stage_c(p, q)
        if p == 0:
            pair[1].wait()
        for q in range(Q):
            stage_d(p, q)
            stage_a(p + 1, q)
        for q in range(Q):
            stage_b(p + 1, q)
    mine = lev_dev * v - base
    for q in range(Q):
        for t in range(tiles_dev):
            for level in range(lev_dev):
                final[core * Q + q, t, level] = halos[STEPS % 2 * Q + q][
                    blk + t * window + mine + level
                ]
    for q in range(Q):
        for copy in last_copies(q):
            copy.wait_recv()
    for level in range(lev_dev):
        for t in range(tiles_dev):
            whole = jnp.concatenate(
                [final[i, t, level] for i in range(2 * Q)], axis=0
            )
            out[level, t * size : (t + 1) * size, :] = whole.T
    for q in range(Q):
        sends_done(STEPS, q)
        for copy in last_copies(q):
            copy.wait_send()


def on_device(h_size, v_size, tracer, tiles, columns, counts, source, implicit, settling, wet):
    lev_dev, cells_dev, classes = tracer.shape
    slots, size = tiles.shape[2], tiles.shape[3]
    tiles_dev = cells_dev // size
    levels = implicit.shape[1]
    share = implicit.shape[0]
    window = lev_dev + 2 * REACH
    assert lev_dev == 2 and tiles_dev == 2 and v_size == 4 and h_size % 2 == 0
    ch = classes // 2 // Q
    flat = implicit.reshape(share, levels * levels).T
    right = lax.rem(lax.axis_index("vert"), 2).astype(F32)
    flat = jnp.concatenate([flat * (1.0 - right), flat * right], axis=1)
    wet_rows = wet.astype(F32).reshape(lev_dev * tiles_dev, size)
    extra = jnp.concatenate([flat, wet_rows, jnp.zeros_like(wet_rows)], axis=0)
    vm = pl.BlockSpec(memory_space=pltpu.VMEM)
    sm = pl.BlockSpec(memory_space=pltpu.SMEM)
    phases = STEPS + 1
    cols = columns.reshape(lev_dev, tiles_dev * slots)
    cols = jnp.pad(cols, ((0, 8 - lev_dev), (0, 128 - cols.shape[1])))
    dma = pltpu.SemaphoreType.DMA
    return pl.pallas_call(
        functools.partial(kernel, h_size, v_size),
        out_shape=jax.ShapeDtypeStruct(tracer.shape, tracer.dtype),
        in_specs=[vm] * 6 + [sm],
        out_specs=vm,
        scratch_shapes=[
            pltpu.VMEM((2 * lev_dev, tiles_dev, slots * size, size), BF16),
            pltpu.VMEM((lev_dev, tiles_dev, classes, size), BF16),
            pltpu.VMEM((2, Q, levels, tiles_dev, ch, size), BF16),
            pltpu.VMEM((Q, lev_dev, tiles_dev, ch, size), BF16),
            pltpu.VMEM((2 * Q, tiles_dev, lev_dev, ch, size), BF16),
            pltpu.VMEM((tiles_dev, classes, size), F32),
            pltpu.VMEM((classes, size), F32),
            pltpu.VMEM((v_size,) + extra.shape, F32),
            pltpu.VMEM((tiles_dev, (window + 1) * levels, size), F32),
            pltpu.VMEM((tiles_dev, 8, size), F32),
            pltpu.VMEM((2,) + cols.shape, jnp.int32),
            pltpu.SMEM((2,) + cols.shape, jnp.int32),
            pltpu.SMEM((2 * lev_dev, tiles_dev * slots), jnp.int32),
            dma((phases, Q, 3)),
            dma((phases, Q, 3)),
            dma((Q, 3)),
            dma((Q, 3)),
            dma((Q, tiles_dev)),
            dma((Q, tiles_dev)),
            dma((3,)),
            dma((3,)),
            dma((2,)),
            dma((2,)),
            dma(()),
        ]
        + [pltpu.VMEM((3 * tiles_dev * window, ch, size), BF16)] * (2 * Q),
        compiler_params=pltpu.CompilerParams(
            collective_id=0, has_side_effects=True, vmem_limit_bytes=32 * 2**20
        ),
    )(tracer, tiles, source, extra, settling.reshape(1, classes), cols, counts)


def solution(mesh):
    placed = (
        P("vert", "horiz", None),
        P("vert", "horiz", None, None, None),
        P("vert", "horiz", None),
        P("vert", "horiz"),
        P("horiz", None),
        P(("horiz", "vert"), None, None),
        P(),
        P("vert", "horiz"),
    )
    body = functools.partial(on_device, mesh.shape["horiz"], mesh.shape["vert"])
    return jax.shard_map(
        body, mesh=mesh, in_specs=placed, out_specs=P("vert", "horiz", None), check_vma=False
    )
```

time: 71.4 us -> 55.9 us (0.78)
  Pallas kernels: 66.4 us -> 51.4 us
    pallas_call x1, Pallas kernels: 66.4 us -> 51.4 us  [on_device(): pl.pallas_call(functools.partial(kernel, h_size, v_size), out_shape=jax.S...]
where the time goes in v2:
time: 55.9 us; the launch traced here: 55.6 us
  Pallas kernels  51.4 us (92%)
  local copies, waits for them, and re-layouts  3.43 us (6%)
  other arithmetic  0.78 us (1%)
    pallas_call x1, Pallas kernels, on_device(): pl.pallas_call(functools.partial(kernel, h_size, v_size), out_shape=jax.S...  51.4 us
    unnamed x13, local copies, waits for them, and re-layouts  2.57 us

profile of v2, /device:TPU:25, one launch (start us, length us, event | category | flops | bytes accessed | tf_op | source)
XLA Modules:
  0.0 55.6 jit_solution(16427221412896914388)
XLA Ops:
  0.0 0.0 copy-start.5
  0.0 0.0 copy-start.1
  0.0 0.1 pad.8.clone
  0.1 0.8 %reshape.16 = s32[2,14]{1,0:T(2,128)S(1)} reshape(s32[2,2,7]{2,1,0:T(2,128)} %param.10) | data formatting | bytes 224 | tf_op jit(solution)/shard_map/reshape | solution.py:388
  0.8 0.7 %convert_element_type.7 = f32[2,256]{1,0:T(2,128)S(1)} convert(s32[2,256]{1,0:T(2,128)} %param.15) | non-fusion elementwise | flops 512 | bytes 4096 | tf_op jit(solution)/shard_map/convert_element_type | solution.py:383
  1.6 0.0 copy-done.5
  1.6 0.0 copy-start.2
  1.6 0.0 copy-start.3
  1.6 0.0 copy-start.4
  1.6 0.1 maximum_maximum_fusion.extra
  1.7 0.0 copy-done.1
  1.7 0.7 %copy-done.2 = bf16[256,128]{1,0:T(8,128)(2,1)S(1)} copy-done((bf16[256,128]{1,0:T(8,128)(2,1)S(1)}, bf16[256,128]{1,0:T(8,128)(2,1)}, u32[]{:S(2)}) %copy-start.2) | copy-done | bytes 65560
  2.4 0.0 copy-done.3
  2.4 0.0 copy-done.4
  2.4 0.0 copy-start
  2.4 1.2 %copy-done = bf16[2,2,7,128,128]{4,3,2,1,0:T(8,128)(2,1)S(1)} copy-done((bf16[2,2,7,128,128]{4,3,2,1,0:T(8,128)(2,1)S(1)}, bf16[2,2,7,128,128]{4,3,2,1,0:T(8,128)(2,1)}, u32[]{:S(2)}) %copy-start) | copy-done | bytes 917528
  3.6 51.4 %shard_map.82 = bf16[2,256,128]{2,1,0:T(8,128)(2,1)S(1)} custom-call(bf16[2,256,128]{2,1,0:T(8,128)(2,1)S(1)} %copy-done.1, bf16[2,2,7,128,128]{4,3,2,1,0:T(8,128)(2,1)S(1)} %copy-done, bf16[256,128]{1,0:T(8,128)(2,1)S(1)} %copy-done.2, f32[72,128]{1,0:T(8,128)S(1)} %maximum_maximum_fusion.extra, f32[1,128]{1,0:T(1,128)S(1)} %bitcast.9, ...), custom_call_target="tpu_custom_call" | custom-call | tf_op jit(solution)/shard_map/pallas_call | solution.py:391
  55.0 0.7 %copy.10 = bf16[2,256,128]{2,1,0:T(8,128)(2,1)} copy(bf16[2,256,128]{2,1,0:T(8,128)(2,1)S(1)} %shard_map.82) | data formatting | bytes 262144
  (4 shorter events, 0.0 us)
Async XLA Ops:
  0.0 1.6 %copy-start.5 = (f32[64,8,8]{0,2,1:T(8,128)S(1)}, f32[64,8,8]{0,2,1:T(8,128)}, u32[]{:S(2)}) copy-start(f32[64,8,8]{0,2,1:T(8,128)} %param.13) | copy-start | bytes 49156
  0.0 1.7 %copy-start.1 = (bf16[2,256,128]{2,1,0:T(8,128)(2,1)S(1)}, bf16[2,256,128]{2,1,0:T(8,128)(2,1)}, u32[]{:S(2)}) copy-start(bf16[2,256,128]{2,1,0:T(8,128)(2,1)} %tracer.1) | copy-start | bytes 393220
  1.6 0.8 %copy-start.2 = (bf16[256,128]{1,0:T(8,128)(2,1)S(1)}, bf16[256,128]{1,0:T(8,128)(2,1)}, u32[]{:S(2)}) copy-start(bf16[256,128]{1,0:T(8,128)(2,1)} %source.1) | copy-start | bytes 196612
  1.6 0.8 %copy-start.3 = (s32[2,2]{1,0:T(2,128)S(1)}, s32[2,2]{1,0:T(2,128)}, u32[]{:S(2)}) copy-start(s32[2,2]{1,0:T(2,128)} %counts.1) | copy-start | bytes 52
  1.6 0.8 %copy-start.4 = (f32[128]{0:T(128)S(1)}, f32[128]{0:T(128)}, u32[]{:S(2)}) copy-start(f32[128]{0:T(128)} %param.14) | copy-start | bytes 1540
  2.4 1.2 %copy-start = (bf16[2,2,7,128,128]{4,3,2,1,0:T(8,128)(2,1)S(1)}, bf16[2,2,7,128,128]{4,3,2,1,0:T(8,128)(2,1)}, u32[]{:S(2)}) copy-start(bf16[2,2,7,128,128]{4,3,2,1,0:T(8,128)(2,1)} %tiles.1) | copy-start | bytes 2752516
